TPU v7x, 32 devices: a whole 2x2x4 slice. The times are simulated.
32 devices in a mesh: tm: 8 (over z, core), head: 4 (over y, x).
Axes of the slice: x: 2, y: 2, z: 4, core: 2. Of those that a mesh axis runs over, the one named last changes fastest.
Arguments:
- frames: bfloat16 [4096, 2048], P(('tm', 'head')), may hold values from -6 to 6
- log_decay: float32 [4096, 16], P('tm', 'head'), may hold values from -2 to 0, as said below
- w_query: bfloat16 [2048, 2048], P('tm', 'head'), may hold values from -0.125 to 0.125
- w_key: bfloat16 [2048, 2048], P('tm', 'head'), may hold values from -0.125 to 0.125
- w_value: bfloat16 [2048, 2048], P('tm', 'head'), may hold values from -0.125 to 0.125
- w_gate: bfloat16 [2048, 2048], P('tm', 'head'), may hold values from -0.125 to 0.125
- w_out: bfloat16 [2048, 2048], P('head', 'tm'), may hold values from -0.125 to 0.125
Outputs:
- mixed: bfloat16 [4096, 2048], P(('tm', 'head'))
Inputs may be any that keep to these rules, and one draw needn't show every extreme that they name: `log_decay`: strictly negative.
All inputs are finite; a program needn't handle non-finite values.
Results may differ from a plain program's by a relative error of at most 0.015.
Values may be sent and summed in bfloat16 or wider, within the bound.
A program may use at most 64 MiB of HBM per device.

v0:
```python
import jax
import jax.numpy as jnp
from jax import lax
from jax.sharding import PartitionSpec as P

HEAD_DIM = 128
BLOCK = 512


def carried_in(value, axis, join, neutral):
    count, mine = (lax.axis_size(axis), lax.axis_index(axis))
    pieces = jax.tree.map(lambda part: lax.all_gather(part, axis), value)
    running = jax.tree.map(
        lambda part, zero: jnp.full_like(part, 0) + jnp.asarray(zero, part.dtype), value, neutral
    )

    def lap(position, running):
        longer = join(running, jax.tree.map(lambda part: part[position], pieces))
        return jax.tree.map(lambda new, old: jnp.where(position < mine, new, old), longer, running)

    return lax.fori_loop(0, count - 1, lap, running)


def combine_states(earlier, later):
    return (earlier[0] * later[0], later[0][:, None, None] * earlier[1] + later[1])


def shards(frames, log_decay, w_query, w_key, w_value, w_gate, w_out):
    rows_query, rows_key, rows_value, rows_gate = (
        lax.all_gather(w_query, "tm", axis=0, tiled=True),
        lax.all_gather(w_key, "tm", axis=0, tiled=True),
        lax.all_gather(w_value, "tm", axis=0, tiled=True),
        lax.all_gather(w_gate, "tm", axis=0, tiled=True),
    )
    joined = jnp.concatenate([rows_query, rows_key, rows_value, rows_gate], axis=1)
    head_width = rows_query.shape[1]
    projected = jnp.dot(
        lax.all_gather(frames, "head", axis=0, tiled=True),
        joined,
        preferred_element_type=jnp.float32,
    )
    local_len = projected.shape[0]
    heads_here = head_width // HEAD_DIM
    block_count = local_len // BLOCK
    query_blocks = (
        projected[:, :head_width]
        .astype(jnp.bfloat16)
        .reshape(block_count, BLOCK, heads_here, HEAD_DIM)
    )
    key_blocks = (
        projected[:, head_width : 2 * head_width]
        .astype(jnp.bfloat16)
        .reshape(block_count, BLOCK, heads_here, HEAD_DIM)
    )
    value_blocks = (
        projected[:, 2 * head_width : 3 * head_width]
        .astype(jnp.bfloat16)
        .reshape(block_count, BLOCK, heads_here, HEAD_DIM)
    )
    gate_all = projected[:, 3 * head_width :]
    running_blocks = jnp.cumsum(log_decay.reshape(block_count, BLOCK, heads_here), axis=1)
    slice_ordinal = jnp.arange(BLOCK, dtype=jnp.int32)
    causal = slice_ordinal[:, None] >= slice_ordinal[None, :]

    def local_step(carry_state, inputs):
        query_block, key_block, value_block, running = inputs
        gaps = running.T[:, :, None] - running.T[:, None, :]
        decay = jnp.exp(jnp.where(causal[None], gaps, -jnp.inf))
        scores = jnp.einsum(
            "thd,shd->hts", query_block, key_block, preferred_element_type=jnp.float32
        )
        weights = (scores * decay).astype(jnp.bfloat16)
        intra = jnp.einsum("hts,shd->thd", weights, value_block, preferred_element_type=jnp.float32)
        scaled = (
            key_block.astype(jnp.float32) * jnp.exp(running[-1][None, :] - running)[:, :, None]
        ).astype(jnp.bfloat16)
        update = jnp.einsum("shd,she->hde", scaled, value_block, preferred_element_type=jnp.float32)
        next_state = jnp.exp(running[-1])[:, None, None] * carry_state + update
        return (next_state, (intra, carry_state))

    zero_state = jnp.zeros((heads_here, HEAD_DIM, HEAD_DIM), jnp.float32)
    local_final, (intra_all, local_starts) = lax.scan(
        local_step, zero_state, (query_blocks, key_blocks, value_blocks, running_blocks)
    )
    decay_total = jnp.exp(jnp.sum(log_decay, axis=0))
    identity = (jnp.ones_like(decay_total), jnp.zeros_like(local_final))
    prior = carried_in((decay_total, local_final), "tm", combine_states, identity)[1]
    block_logs = running_blocks[:, -1, :]
    before = jnp.cumsum(block_logs, axis=0) - block_logs
    start_states = jnp.exp(before)[:, :, None, None] * prior[None] + local_starts
    lifted = query_blocks.astype(jnp.float32) * jnp.exp(running_blocks)[..., None]
    inter = jnp.einsum("cthd,chde->cthe", lifted, start_states, precision=lax.Precision.HIGHEST)
    retained = (intra_all + inter).reshape(local_len, heads_here, HEAD_DIM)
    center = jnp.mean(retained, axis=-1, keepdims=True)
    spread = jnp.mean((retained - center) ** 2, axis=-1, keepdims=True)
    normed = (retained - center) / jnp.sqrt(spread + 1e-05)
    gated = (
        (jax.nn.silu(gate_all.reshape(local_len, heads_here, HEAD_DIM)) * normed)
        .astype(jnp.bfloat16)
        .reshape(local_len, head_width)
    )
    owned = lax.all_to_all(gated, "head", split_axis=0, concat_axis=1, tiled=True)
    rows_out = lax.all_gather(w_out, "tm", axis=1, tiled=True)
    return jnp.dot(
        owned,
        lax.all_gather(rows_out, "head", axis=0, tiled=True),
        preferred_element_type=jnp.float32,
    ).astype(jnp.bfloat16)


def solution(mesh):
    return jax.shard_map(
        shards,
        mesh=mesh,
        in_specs=(
            P(("tm", "head"), None),
            P("tm", "head"),
            P("tm", "head"),
            P("tm", "head"),
            P("tm", "head"),
            P("tm", "head"),
            P("head", "tm"),
        ),
        out_specs=P(("tm", "head"), None),
        check_vma=False,
    )
```

profile of v0, /device:TPU:29, one launch (start us, length us, event | category | flops | bytes accessed | tf_op | source)
XLA Modules:
  0.0 335.2 jit_solution(16961226316841263543)
XLA Ops:
  6.5 0.7 all-gather.19.cloned.1.call-update
  7.3 0.7 all-gather.17.cloned.1.call-update
  8.1 0.7 all-gather.15.cloned.1.call-update
  8.8 0.5 all-gather.13.cloned.1.call-update
  9.4 0.5 all-gather.11.cloned.1.call-update
  9.9 0.5 all-gather.21.cloned.1.call-update
  10.5 0.0 all-gather.25.cloned.1.call-start
  10.5 0.7 reshape.149
  11.2 1.2 reduce-window.6
  12.5 0.2 slice_reduce_fusion
  12.6 0.2 reduce-window.9
  12.8 0.1 broadcast.65
  12.9 0.2 slice_reduce_fusion.1
  13.1 0.1 fusion.25
  13.2 32.3 %all-gather.19.cloned.1.call-done = bf16[512,2048]{1,0:T(8,128)(2,1)} async-done(((bf16[128,2048]{1,0:T(8,128)(2,1)}), bf16[512,2048]{1,0:T(8,128)(2,1)}) %all-gather.19.cloned.1.call-update) | async-done | bytes 2097168 | tf_op jit(solution)/shard_map/all_gather | solution.py:38
  45.5 29.7 %all-gather.17.cloned.1.call-done = bf16[2048,512]{1,0:T(8,128)(2,1)} async-done(((bf16[256,512]{1,0:T(8,128)(2,1)}), bf16[2048,512]{1,0:T(8,128)(2,1)}) %all-gather.17.cloned.1.call-update) | async-done | bytes 2097168 | tf_op jit(solution)/shard_map/all_gather | solution.py:33
  75.2 30.2 %all-gather.15.cloned.1.call-done = bf16[2048,512]{1,0:T(8,128)(2,1)} async-done(((bf16[256,512]{1,0:T(8,128)(2,1)}), bf16[2048,512]{1,0:T(8,128)(2,1)}) %all-gather.15.cloned.1.call-update) | async-done | bytes 2097168 | tf_op jit(solution)/shard_map/all_gather | solution.py:32
  105.4 30.1 %all-gather.13.cloned.1.call-done = bf16[2048,512]{1,0:T(8,128)(2,1)} async-done(((bf16[256,512]{1,0:T(8,128)(2,1)}), bf16[2048,512]{1,0:T(8,128)(2,1)}) %all-gather.13.cloned.1.call-update) | async-done | bytes 2097168 | tf_op jit(solution)/shard_map/all_gather | solution.py:31
  135.5 30.1 %all-gather.11.cloned.1.call-done = bf16[2048,512]{1,0:T(8,128)(2,1)} async-done(((bf16[256,512]{1,0:T(8,128)(2,1)}), bf16[2048,512]{1,0:T(8,128)(2,1)}) %all-gather.11.cloned.1.call-update) | async-done | bytes 2097168 | tf_op jit(solution)/shard_map/all_gather | solution.py:30
  165.6 10.1 %fusion.29 = (bf16[512,2048]{0,1:T(8,128)(2,1)S(1)}, f32[512,2048]{0,1:T(8,128)}) fusion(bf16[512,2048]{1,0:T(8,128)(2,1)} %all-gather.19.cloned.1.call-done, bf16[2048,512]{1,0:T(8,128)(2,1)} %all-gather.17.cloned.1.call-done, bf16[2048,512]{1,0:T(8,128)(2,1)} %all-gather.15.cloned.1.call-done, bf16[2048,512]{1,0:T(8,128)(2,1)} %all-gather.13.cloned.1.call-done, ...), kind=kOutput, calls=%fused_computation.49 | convolution fusion | flops 4329570304 | bytes 16777216 | tf_op jit(solution)/shard_map/dot_general | solution.py:37
  175.6 0.1 fusion.28
  175.7 1.0 convolution_add_fusion
  176.8 0.0 all-gather.23.cloned.1.call-start
  176.8 19.7 %all-gather.21.cloned.1.call-done = bf16[512,2048]{1,0:T(8,128)(2,1)} async-done(((bf16[512,256]{1,0:T(8,128)(2,1)}), bf16[512,2048]{1,0:T(8,128)(2,1)}) %all-gather.21.cloned.1.call-update) | async-done | bytes 2097168 | tf_op jit(solution)/shard_map/all_gather | solution.py:103
  196.6 0.1 reduce_sum.27
  196.7 0.6 dynamic-slice.1
  198.0 0.1 exponential_dynamic-update-slice_fusion
  198.1 13.1 %all-reduce = f32[32]{0:T(128)S(1)} all-reduce(f32[32]{0:T(128)S(1)} %exponential_dynamic-update-slice_fusion), channel_id=2, replica_groups=mesh['tm'=8,'head'=4] {'tm'}, use_global_device_ids=true, to_apply=%add | all-reduce | flops 32 | bytes 256
  211.3 0.1 reshape.156
  211.3 0.1 iota_compare_fusion
  211.4 0.3 copy.48
  211.7 15.6 %all-gather.25.cloned.1.call-done = f32[32,128,128]{2,1,0:T(8,128)} async-done(((f32[4,128,128]{2,1,0:T(8,128)}), f32[32,128,128]{2,1,0:T(8,128)}) %all-gather.25.cloned.1.call-update) | async-done | bytes 2097168 | tf_op jit(solution)/shard_map/all_gather | solution.py:12
  227.3 7.6 %while.9 = (s32[]{:T(128)}, f32[4,128,128]{2,1,0:T(8,128)S(1)}, s32[]{:T(128)}, f32[8,4]{1,0:T(8,128)S(1)}, f32[8,4,128,128]{3,2,1,0:T(8,128)}, /*index=5*/s32[]{:T(128)}, s32[]{:T(128)}) while((s32[]{:T(128)}, f32[4,128,128]{2,1,0:T(8,128)S(1)}, s32[]{:T(128)}, f32[8,4]{1,0:T(8,128)S(1)}, f32[8,4,128,128]{3,2,1,0:T(8,128)}, ...), condition=%wide.region_4.5_spmd.clone, body=%wide.region_3.4_spmd.clone.sunk | while | flops 262148 | bytes 786593 | solution.py:21
  227.3 1.0 fusion.40
  228.4 1.1 fusion.40
  229.4 1.1 fusion.40
  230.5 1.1 fusion.40
  231.6 1.1 fusion.40
  232.7 1.1 fusion.40
  233.8 1.1 fusion.40
  234.9 2.5 convolution_bitcast_fusion
  237.4 3.4 %fusion.30 = (f32[512,4]{0,1:T(4,128)S(1)}, f32[1,512,4,128]{1,3,2,0:T(8,128)S(1)}) fusion(f32[1,512,4,128]{1,3,2,0:T(8,128)} %convolution_bitcast_fusion, bf16[512,4,128]{0,2,1:T(8,128)(2,1)S(1)} %bitcast.81, bf16[512,4,128]{0,2,1:T(8,128)(2,1)S(1)} %bitcast.83, bf16[512,4,128]{0,2,1:T(8,128)(2,1)S(1)} %bitcast.79, f32[4,512]{1,0:T(4,128)S(1)} %bitcast.86, ...), kind=kOutput, calls=%fused_computation.50 | convolution fusion | flops 541587456 | bytes 3948544 | tf_op jit(solution)/shard_map/while/body/eval_jaxpr/hts,shd->thd/dot_general | solution.py:73
  240.8 0.1 fusion.18
  241.0 1.8 fusion.16
  242.8 0.1 copy_bitcast_fusion
  242.9 17.0 %all_to_all.19 = bf16[4,128,512]{1,2,0:T(8,128)(2,1)S(1)} all-to-all(bf16[4,128,512]{1,2,0:T(8,128)(2,1)S(1)} %copy_bitcast_fusion), channel_id=1, replica_groups=mesh['tm'=8,'head'=4] {'head'}, dimensions={0} | all-to-all | bytes 1048576 | tf_op jit(solution)/shard_map/all_to_all | solution.py:102
  260.0 62.9 %all-gather.23.cloned.1.call-done = bf16[2048,2048]{1,0:T(8,128)(2,1)} async-done(((bf16[512,2048]{1,0:T(8,128)(2,1)}), bf16[2048,2048]{1,0:T(8,128)(2,1)}) %all-gather.23.cloned.1.call-update) | async-done | bytes 8388624 | tf_op jit(solution)/shard_map/all_gather | solution.py:106
  322.9 5.5 %convolution_convert_fusion = bf16[128,2048]{1,0:T(8,128)(2,1)} fusion(bf16[128,2048]{0,1:T(8,128)(2,1)S(1)} %bitcast.77, bf16[2048,2048]{1,0:T(8,128)(2,1)} %all-gather.23.cloned.1.call-done), kind=kOutput, calls=%fused_computation.13 | convolution fusion | flops 1074003968 | bytes 9437184 | tf_op jit(solution)/shard_map/dot_general | solution.py:104
  (28 shorter events, 0.4 us)
Async XLA Ops:
  6.5 38.9 %all-gather.19.cloned.1.call-start = ((), (), s32[]{:S(2)}) async-start(), calls=%async_computation.5 | async-start | bytes 2621440 | tf_op jit(solution)/shard_map/all_gather | solution.py:38
  7.3 67.9 %all-gather.17.cloned.1.call-start = ((), (), s32[]{:S(2)}) async-start(), calls=%async_computation.4 | async-start | bytes 2359296 | tf_op jit(solution)/shard_map/all_gather | solution.py:33
  8.0 97.4 %all-gather.15.cloned.1.call-start = ((), (), s32[]{:S(2)}) async-start(), calls=%async_computation.3 | async-start | bytes 2359296 | tf_op jit(solution)/shard_map/all_gather | solution.py:32
  8.7 126.8 %all-gather.13.cloned.1.call-start = ((), (), s32[]{:S(2)}) async-start(), calls=%async_computation.2 | async-start | bytes 2359296 | tf_op jit(solution)/shard_map/all_gather | solution.py:31
  9.3 156.3 %all-gather.11.cloned.1.call-start = ((), (), s32[]{:S(2)}) async-start(), calls=%async_computation.1 | async-start | bytes 2359296 | tf_op jit(solution)/shard_map/all_gather | solution.py:30
  9.9 186.7 %all-gather.21.cloned.1.call-start = ((), (), s32[]{:S(2)}) async-start(), calls=%async_computation.6 | async-start | bytes 2359296 | tf_op jit(solution)/shard_map/all_gather | solution.py:103
  10.5 216.8 %all-gather.25.cloned.1.call-start = ((), (), s32[]{:S(2)}) async-start(), calls=%async_computation.8 | async-start | bytes 2359296 | tf_op jit(solution)/shard_map/all_gather | solution.py:12
  175.6 21.0 %copy-start = (f32[512,4]{0,1:T(4,128)S(1)}, f32[512,4]{0,1:T(4,128)}, u32[]{:S(2)}) copy-start(f32[512,4]{0,1:T(4,128)} %param.10) | copy-start | bytes 24580
  175.6 21.1 %copy-start.1 = (u32[32]{0:T(128)S(1)}, u32[32]{0:T(128)}, u32[]{:S(2)}) copy-start(u32[32]{0:T(128)} %constant.69) | copy-start | bytes 388
  176.8 146.1 %all-gather.23.cloned.1.call-start = ((), (), s32[]{:S(2)}) async-start(), calls=%async_computation.7 | async-start | bytes 10485760 | tf_op jit(solution)/shard_map/all_gather | solution.py:106
Sparse Core Ops, SparseCore 0:
  9.2 36.2 all-gather.18
  47.1 28.0 all-gather.16
  76.8 28.5 all-gather.14
  106.9 28.5 all-gather.12
  136.9 28.5 all-gather.10
  167.0 29.4 all-gather.20
  198.2 29.0 all-gather.24
  229.1 93.7 all-gather.22
where the time goes:
time: 338 us; the launch traced here: 335 us
  waiting for transfers between devices  254 us (75%)
  blocking collectives  30.2 us (9%)
  matrix products  22.4 us (7%)
  between operations  14.2 us (4%)
  other arithmetic  11 us (3%)
    all_gather x1, waiting for transfers between devices, shards(): lax.all_gather(rows_out, 'head', axis=0, tiled=True)  62.9 us
    all_gather x1, waiting for transfers between devices, shards(): lax.all_gather(frames, 'head', axis=0, tiled=True)  32.3 us
    all_gather x1, waiting for transfers between devices, shards(): lax.all_gather(w_value, 'tm', axis=0, tiled=True)  30.2 us
    all_gather x1, waiting for transfers between devices, shards(): lax.all_gather(w_key, 'tm', axis=0, tiled=True)  30.1 us
    all_gather x1, waiting for transfers between devices, shards(): lax.all_gather(w_query, 'tm', axis=0, tiled=True)  30.1 us
    all_gather x1, waiting for transfers between devices, shards(): lax.all_gather(w_gate, 'tm', axis=0, tiled=True)  29.7 us
    all_gather x1, waiting for transfers between devices, shards(): rows_out = lax.all_gather(w_out, 'tm', axis=1, tiled=True)  19.7 us
    all_to_all x1, blocking collectives, shards(): lax.all_to_all(gated, 'head', split_axis=0, concat_axis=1, tiled=True)  17 us
  transfers between devices with their start and end apart: 8, of which 8 were waited for; matrix products, arithmetic and copies ran while one was open for 9% of the time, Pallas kernels for 0%

commit v1 on v0

v1 whole, which is shorter than its diff:
```python
import functools

import jax
import jax.numpy as jnp
from jax import lax
from jax.experimental import pallas as pl
from jax.experimental.pallas import tpu as pltpu
from jax.sharding import PartitionSpec as P

HEAD_DIM = 128
MESH = pl.DeviceIdType.MESH
F32 = jnp.float32
BF16 = jnp.bfloat16


def kernel(
    tms, heads_axis, x_ref, ld_ref, wk_ref, wv_ref, wq_ref, wg_ref, wo_ref, out_ref,
    x, w, wo, acc, decay, runs, sown, sprev, rin, rout, ret, gated, owned,
    x_send, x_recv, w_send, w_recv, o_recv, oxy_send, osib_send,
    s_send, s_recv, r_send, r_recv, rs_send, g_send, g_recv,
):
    zs = tms // 2
    tm, hd = lax.axis_index("tm"), lax.axis_index("head")
    z, c = lax.div(tm, 2), lax.rem(tm, 2)
    sibling = (2 * z + 1 - c, hd)
    rows = wk_ref.shape[0]
    width = wk_ref.shape[1]
    frames_here = x_ref.shape[0]
    length = frames_here * heads_axis
    heads = width // HEAD_DIM

    def peer(p):
        return lax.rem(hd + p, heads_axis)

    def remote(ref_from, ref_to, send, recv, device):
        return pltpu.make_async_remote_copy(
            src_ref=ref_from, dst_ref=ref_to, send_sem=send, recv_sem=recv,
            device_id=device, device_id_type=MESH,
        )

    def slot(m, position):
        if m == 0:
            return wo.at[hd, position], o_recv.at[hd, position]
        return w.at[m - 1, position], w_recv.at[m - 1, position]

    def along(m, zo, side):
        ref, recv = slot(m, 2 * zo + c)
        to = z + 1 - 2 * side
        return remote(ref, ref, w_send.at[m, zo, side], recv, (2 * to + c, hd))

    def across(m, zo):
        ref, recv = slot(m, 2 * zo + c)
        return remote(ref, ref, w_send.at[m, zo, 2], recv, sibling)

    def landed(m, position):
        ref, recv = slot(m, position)
        remote(ref, ref, w_send.at[m, 0, 2], recv, sibling).wait_recv()

    def plane(zo, p):
        ref = wo.at[hd, 2 * zo + c]
        return remote(ref, ref, oxy_send.at[zo, p], o_recv.at[hd, 2 * zo + c], (tm, peer(p)))

    def plane_across(zo, p):
        at = peer(p)
        ref = wo.at[at, 2 * zo + c]
        return remote(ref, ref, osib_send.at[zo, p], o_recv.at[at, 2 * zo + c], sibling)

    def out_landed(at, position):
        ref = wo.at[at, position]
        remote(ref, ref, osib_send.at[0, 0], o_recv.at[at, position], sibling).wait_recv()

    def both(d, body):
        def one(side, _):
            zo = z - d + 2 * d * side
            first = jnp.logical_or(side == 0, d > 0)

            @pl.when(jnp.logical_and(first, jnp.logical_and(zo >= 0, zo < zs)))
            def _():
                body(zo, side)

            return 0

        lax.fori_loop(0, 2, one, 0)

    def pass_on(m, d):
        def body(zo, side):
            landed(m, 2 * zo + c)
            to = z + 1 - 2 * side

            @pl.when(jnp.logical_and(to >= 0, to < zs))
            def _():
                along(m, zo, side).start()

            across(m, zo).start()
            if m == 0:
                for p in range(1, heads_axis):
                    plane(zo, p).start()

        both(d, body)

    def project(m, d):
        def body(zo, side):
            landed(m, 2 * zo + 1 - c)
            columns = pl.ds(pl.multiple_of(zo * (2 * rows), 2 * rows), 2 * rows)
            block = w[m - 1, pl.ds(2 * zo, 2)].reshape(2 * rows, width)
            acc[m - 1] += jnp.dot(x[:, columns], block, preferred_element_type=F32)

        both(d, body)

    def plane_pass_on(d):
        def body(zo, side):
            for p in range(1, heads_axis):
                out_landed(peer(p), 2 * zo + c)
                plane_across(zo, p).start()

        both(d, body)

    barrier = pltpu.get_barrier_semaphore()
    pl.semaphore_signal(barrier, inc=1, device_id=sibling, device_id_type=MESH)
    for p in range(1, heads_axis):
        pl.semaphore_signal(barrier, inc=1, device_id=(tm, peer(p)), device_id_type=MESH)

    @pl.when(z > 0)
    def _():
        pl.semaphore_signal(barrier, inc=1, device_id=(tm - 2, hd), device_id_type=MESH)

    @pl.when(z < zs - 1)
    def _():
        pl.semaphore_signal(barrier, inc=1, device_id=(tm + 2, hd), device_id_type=MESH)

    here = pl.ds(pl.multiple_of(hd * frames_here, frames_here), frames_here)
    x[here, :] = x_ref[...]
    wo[hd, tm] = wo_ref[...]
    for m, ref in enumerate((wk_ref, wv_ref, wq_ref, wg_ref)):
        w[m, tm] = ref[...]
    neighbours = (z > 0).astype(jnp.int32) + (z < zs - 1).astype(jnp.int32)
    pl.semaphore_wait(barrier, heads_axis + neighbours)

    def x_copy(p):
        return remote(x.at[here, :], x.at[here, :], x_send.at[p], x_recv.at[hd], (tm, peer(p)))

    for p in range(1, heads_axis):
        x_copy(p).start()
    for m in range(5):

        @pl.when(z < zs - 1)
        def _():
            along(m, z, 0).start()

        @pl.when(z > 0)
        def _():
            along(m, z, 1).start()

        across(m, z).start()
        if m == 0:
            for p in range(1, heads_axis):
                plane(z, p).start()

    acc[...] = jnp.zeros_like(acc)
    at_row = lax.broadcasted_iota(jnp.int32, (length, length), 0)
    at_col = lax.broadcasted_iota(jnp.int32, (length, length), 1)
    for h in range(heads):
        steps = ld_ref[:, h : h + 1]
        run_row = jnp.sum(jnp.where(at_row <= at_col, steps, 0.0), axis=0, keepdims=True)
        run_col = jnp.sum(jnp.where(at_row == at_col, run_row, 0.0), axis=1, keepdims=True)
        runs[h] = jnp.broadcast_to(run_col, (length, HEAD_DIM))
        decay[h] = jnp.exp(jnp.where(at_row >= at_col, run_col - run_row, -jnp.inf))
    for p in range(1, heads_axis):
        at = peer(p)
        ref = x.at[pl.ds(pl.multiple_of(at * frames_here, frames_here), frames_here), :]
        remote(ref, ref, x_send.at[p], x_recv.at[at], sibling).wait_recv()

    def lap(d, _):
        for m in range(5):
            pass_on(m, d)
            if m > 0:
                project(m, d - 1)
        plane_pass_on(d - 1)
        return 0

    lax.fori_loop(1, zs - 1, lap, 0)
    for m in range(3):
        pass_on(m, zs - 1)
        if m > 0:
            project(m, zs - 2)
            project(m, zs - 1)

    def columns_of(h):
        return slice(h * HEAD_DIM, (h + 1) * HEAD_DIM)

    def first_copy(h):
        return remote(sown.at[h], sprev.at[h], s_send.at[h], s_recv.at[h], sibling)

    def next_copy(h):
        return remote(rout.at[h], rin.at[h], r_send.at[h], r_recv.at[h], (tm + 2, hd))

    def share_copy(h):
        return remote(rin.at[h], rin.at[h], rs_send.at[h], r_recv.at[h], sibling)

    def state_step(h):
        prior = jnp.exp(sprev[h, HEAD_DIM : HEAD_DIM + 1, :]) * rin[h] + sprev[h, :HEAD_DIM, :]
        rout[h] = jnp.exp(sown[h, HEAD_DIM : HEAD_DIM + 1, :]) * prior + sown[h, :HEAD_DIM, :]
        return prior

    @pl.when(z == 0)
    def _():
        rin[...] = jnp.zeros_like(rin)

    for h in range(heads):
        run = runs[h]
        last = run[length - 1 :, :]
        key = acc[0, :, columns_of(h)].astype(BF16)
        value = acc[1, :, columns_of(h)].astype(BF16)
        scaled = (key.astype(F32) * jnp.exp(last - run)).astype(BF16)
        sown[h, :HEAD_DIM, :] = lax.dot_general(
            scaled, value, (((0,), (0,)), ((), ())), preferred_element_type=F32
        )
        sown[h, HEAD_DIM:, :] = jnp.broadcast_to(last, (8, HEAD_DIM))

        @pl.when(c == 0)
        def _():
            first_copy(h).start()

    @pl.when(jnp.logical_and(c == 1, z == 0))
    def _():
        for h in range(heads):
            first_copy(h).wait_recv()
            state_step(h)
            next_copy(h).start()

    pass_on(3, zs - 1)
    project(3, zs - 2)
    project(3, zs - 1)
    for h in range(heads):
        query = acc[2, :, columns_of(h)].astype(BF16)
        key = acc[0, :, columns_of(h)].astype(BF16)
        value = acc[1, :, columns_of(h)].astype(BF16)
        scores = lax.dot_general(query, key, (((1,), (1,)), ((), ())), preferred_element_type=F32)
        weights = (scores * decay[h]).astype(BF16)
        ret[:, columns_of(h)] = jnp.dot(weights, value, preferred_element_type=F32)
    plane_pass_on(zs - 2)
    pass_on(4, zs - 1)
    project(4, zs - 2)

    @pl.when(jnp.logical_and(c == 1, z > 0))
    def _():
        for h in range(heads):
            first_copy(h).wait_recv()
        for h in range(heads):
            next_copy(h).wait_recv()
            state_step(h)

            @pl.when(z < zs - 1)
            def _():
                next_copy(h).start()

            share_copy(h).start()

    @pl.when(jnp.logical_and(c == 0, z > 0))
    def _():
        for h in range(heads):
            share_copy(h).wait_recv()

    for h in range(heads):

        @pl.when(c == 1)
        def _():
            rout[heads + h] = (
                jnp.exp(sprev[h, HEAD_DIM : HEAD_DIM + 1, :]) * rin[h] + sprev[h, :HEAD_DIM, :]
            )

        @pl.when(c == 0)
        def _():
            rout[heads + h] = rin[h]

        query = acc[2, :, columns_of(h)].astype(BF16)
        lifted = query.astype(F32) * jnp.exp(runs[h])
        both_parts = ret[:, columns_of(h)] + jnp.dot(
            lifted, rout[heads + h], preferred_element_type=F32, precision=lax.Precision.HIGHEST
        )
        centred = both_parts - jnp.mean(both_parts, axis=1, keepdims=True)
        spread = jnp.mean(centred * centred, axis=1, keepdims=True)
        ret[:, columns_of(h)] = centred * lax.rsqrt(spread + 1e-05)

    project(4, zs - 1)

    def g_copy(p):
        at = peer(p)
        piece = gated.at[pl.ds(pl.multiple_of(at * frames_here, frames_here), frames_here), :]
        return remote(piece, owned.at[hd], g_send.at[p], g_recv.at[hd], (tm, at))

    def gate_rows(at):
        part = pl.ds(pl.multiple_of(at * frames_here, frames_here), frames_here)
        gate = acc[3, part, :]
        return (gate / (1.0 + jnp.exp(-gate)) * ret[part, :]).astype(BF16)

    for p in range(1, heads_axis):
        at = peer(p)
        part = pl.ds(pl.multiple_of(at * frames_here, frames_here), frames_here)
        gated[part, :] = gate_rows(at)
        g_copy(p).start()
    owned[hd] = gate_rows(hd)

    plane_pass_on(zs - 1)

    def all_out(zo, _):
        for at in range(heads_axis):
            out_landed(at, 2 * zo + 1 - c)
        return 0

    lax.fori_loop(0, zs, all_out, 0)
    for p in range(1, heads_axis):
        at = peer(p)
        remote(owned.at[at], owned.at[at], g_send.at[p], g_recv.at[at], sibling).wait_recv()

    wide = wo_ref.shape[1]

    def finish(t, _):
        total = jnp.zeros((frames_here, wide), F32)
        for at in range(heads_axis):
            total += jnp.dot(owned[at], wo[at, t], preferred_element_type=F32)
        out_ref[:, pl.ds(pl.multiple_of(t * wide, wide), wide)] = total.astype(BF16)
        return 0

    lax.fori_loop(0, tms, finish, 0)

    for p in range(1, heads_axis):
        x_copy(p).wait_send()
        g_copy(p).wait_send()

    @pl.when(c == 0)
    def _():
        for h in range(heads):
            first_copy(h).wait_send()

    @pl.when(c == 1)
    def _():
        for h in range(heads):

            @pl.when(z < zs - 1)
            def _():
                next_copy(h).wait_send()

            @pl.when(z > 0)
            def _():
                share_copy(h).wait_send()

    def drain(zo, _):
        for m in range(5):
            across(m, zo).wait_send()

            @pl.when(jnp.logical_and(zo <= z, z < zs - 1))
            def _():
                along(m, zo, 0).wait_send()

            @pl.when(jnp.logical_and(zo >= z, z > 0))
            def _():
                along(m, zo, 1).wait_send()

        for p in range(1, heads_axis):
            plane(zo, p).wait_send()
            plane_across(zo, p).wait_send()
        return 0

    lax.fori_loop(0, zs, drain, 0)


def solution(mesh):
    tms, heads_axis = mesh.shape["tm"], mesh.shape["head"]
    zs = tms // 2

    def shards(frames, log_decay, w_query, w_key, w_value, w_gate, w_out):
        here, model = frames.shape
        rows, width = w_query.shape
        length, heads = log_decay.shape
        vmem = pl.BlockSpec(memory_space=pltpu.VMEM)
        dma = pltpu.SemaphoreType.DMA
        return pl.pallas_call(
            functools.partial(kernel, tms, heads_axis),
            out_shape=jax.ShapeDtypeStruct((here, model), BF16),
            in_specs=[vmem] * 7,
            out_specs=vmem,
            scratch_shapes=[
                pltpu.VMEM((length, model), BF16),
                pltpu.VMEM((4, tms, rows, width), BF16),
                pltpu.VMEM((heads_axis, tms) + w_out.shape, BF16),
                pltpu.VMEM((4, length, width), F32),
                pltpu.VMEM((heads, length, length), F32),
                pltpu.VMEM((heads, length, HEAD_DIM), F32),
                pltpu.VMEM((heads, HEAD_DIM + 8, HEAD_DIM), F32),
                pltpu.VMEM((heads, HEAD_DIM + 8, HEAD_DIM), F32),
                pltpu.VMEM((heads, HEAD_DIM, HEAD_DIM), F32),
                pltpu.VMEM((2 * heads, HEAD_DIM, HEAD_DIM), F32),
                pltpu.VMEM((length, width), F32),
                pltpu.VMEM((length, width), BF16),
                pltpu.VMEM((heads_axis, here, width), BF16),
                dma((heads_axis,)),
                dma((heads_axis,)),
                dma((5, zs, 3)),
                dma((4, tms)),
                dma((heads_axis, tms)),
                dma((zs, heads_axis)),
                dma((zs, heads_axis)),
                dma((heads,)),
                dma((heads,)),
                dma((heads,)),
                dma((heads,)),
                dma((heads,)),
                dma((heads_axis,)),
                dma((heads_axis,)),
            ],
            compiler_params=pltpu.CompilerParams(
                collective_id=0, has_side_effects=True, vmem_limit_bytes=50 * 2**20
            ),
        )(frames, log_decay, w_key, w_value, w_query, w_gate, w_out)

    return jax.shard_map(
        shards,
        mesh=mesh,
        in_specs=(
            P(("tm", "head"), None),
            P("tm", "head"),
            P("tm", "head"),
            P("tm", "head"),
            P("tm", "head"),
            P("tm", "head"),
            P("head", "tm"),
        ),
        out_specs=P(("tm", "head"), None),
        check_vma=False,
    )
```

time: 338 us -> 112 us (0.33)
  waiting for transfers between devices: 254 us -> 0 us
  Pallas kernels: 0 us -> 105 us
  blocking collectives: 30.2 us -> 0 us
  matrix products: 22.4 us -> 0 us
  between operations: 14.2 us -> 0.02 us
  other arithmetic: 11 us -> 0 us
  local copies, waits for them, and re-layouts: 2.52 us -> 6.59 us
    all_gather x8 -> x0, waiting for transfers between devices: 251 us -> none  [the longest x1 62.9 us: shards(): lax.all_gather(rows_out, 'head', axis=0, tiled=True)]
    pallas_call x0 -> x1, Pallas kernels: none -> 105 us  [shards(): pl.pallas_call(functools.partial(kernel, tms, heads_axis), out_shape=jax....]
    dot_general x5 -> x0, matrix products: 22.4 us -> none  [the longest x1 10.1 us: shards(): jnp.dot(lax.all_gather(frames, 'head', axis=0, tiled=True), joined, prefe...]
    all_to_all x1 -> x0, blocking collectives: 17 us -> none  [shards(): lax.all_to_all(gated, 'head', split_axis=0, concat_axis=1, tiled=True)]
    unnamed x1 -> x0, blocking collectives: 13.1 us -> none
    select_n x7 -> x0, other arithmetic: 7.36 us -> none  [lap(): jnp.where(position < mine, new, old)]
    unnamed x7 -> x14, local copies, waits for them, and re-layouts: 0.75 us -> 6.59 us
    unnamed x8 -> x0, waiting for transfers between devices: 3.7 us -> none
  transfers between devices with their start and end apart: 8 -> 0, of which waited for: 8 -> 0; matrix products, arithmetic and copies ran while one was open for 9% -> 0% of each run, Pallas kernels for 0% -> 0%
where the time goes in v1:
time: 112 us
  Pallas kernels  105 us (94%)
  local copies, waits for them, and re-layouts  6.59 us (6%)
    pallas_call x1, Pallas kernels, shards(): pl.pallas_call(functools.partial(kernel, tms, heads_axis), out_shape=jax....  105 us
    unnamed x14, local copies, waits for them, and re-layouts  6.59 us

profile of v1, /device:TPU:29, one launch (start us, length us, event | category | flops | bytes accessed | tf_op | source)
XLA Modules:
  0.0 111.9 jit_solution(10748310627298133351)
XLA Ops:
  0.0 0.0 copy-start.1
  0.0 0.9 copy.8.ld_ref
  0.9 0.1 copy-done.1
  1.0 0.0 copy-start
  1.0 1.0 copy-done
  2.0 0.0 copy-start.2
  2.0 0.9 copy-done.2
  3.0 0.0 copy-start.3
  3.0 0.9 copy-done.3
  3.9 0.0 copy-start.4
  3.9 0.9 copy-done.4
  4.9 0.0 copy-start.5
  4.9 0.9 copy-done.5
  5.8 105.2 %shard_map.73 = bf16[128,2048]{1,0:T(8,128)(2,1)S(1)} custom-call(bf16[128,2048]{1,0:T(8,128)(2,1)S(1)} %copy-done, f32[512,4]{1,0:T(8,128)S(1)} %copy.8.ld_ref, bf16[256,512]{1,0:T(8,128)(2,1)S(1)} %copy-done.1, bf16[256,512]{1,0:T(8,128)(2,1)S(1)} %copy-done.2, bf16[256,512]{1,0:T(8,128)(2,1)S(1)} %copy-done.3, bf16[256,512]{1,0:T(8,128)(2,1)S(1)} %copy-done.4, ...), custom_call_target="tpu_custom_call" | custom-call | tf_op jit(solution)/shard_map/pallas_call | solution.py:378
  111.1 0.8 copy.10
Async XLA Ops:
  0.0 1.0 copy-start.1
  1.0 1.0 copy-start
  2.0 0.9 copy-start.2
  3.0 0.9 copy-start.3
  3.9 0.9 copy-start.4
  4.9 0.9 copy-start.5

commit v2 on v1

--- a/solution.py
+++ b/solution.py
@@ -15,7 +15,7 @@
 
 def kernel(
     tms, heads_axis, x_ref, ld_ref, wk_ref, wv_ref, wq_ref, wg_ref, wo_ref, out_ref,
-    x, w, wo, acc, decay, runs, sown, sprev, rin, rout, ret, gated, owned,
+    in_sem, x, w, wo, acc, decay, runs, sown, sprev, rin, rout, ret, gated, owned,
     x_send, x_recv, w_send, w_recv, o_recv, oxy_send, osib_send,
     s_send, s_recv, r_send, r_recv, rs_send, g_send, g_recv,
 ):
@@ -129,19 +129,24 @@
         pl.semaphore_signal(barrier, inc=1, device_id=(tm + 2, hd), device_id_type=MESH)
 
     here = pl.ds(pl.multiple_of(hd * frames_here, frames_here), frames_here)
-    x[here, :] = x_ref[...]
-    wo[hd, tm] = wo_ref[...]
-    for m, ref in enumerate((wk_ref, wv_ref, wq_ref, wg_ref)):
-        w[m, tm] = ref[...]
+    own = [
+        pltpu.make_async_copy(wo_ref, wo.at[hd, tm], in_sem.at[0]),
+        pltpu.make_async_copy(wk_ref, w.at[0, tm], in_sem.at[1]),
+        pltpu.make_async_copy(wv_ref, w.at[1, tm], in_sem.at[2]),
+        pltpu.make_async_copy(wq_ref, w.at[2, tm], in_sem.at[3]),
+        pltpu.make_async_copy(wg_ref, w.at[3, tm], in_sem.at[4]),
+        pltpu.make_async_copy(x_ref, x.at[here, :], in_sem.at[5]),
+    ]
+    for copy in own:
+        copy.start()
     neighbours = (z > 0).astype(jnp.int32) + (z < zs - 1).astype(jnp.int32)
     pl.semaphore_wait(barrier, heads_axis + neighbours)
 
     def x_copy(p):
         return remote(x.at[here, :], x.at[here, :], x_send.at[p], x_recv.at[hd], (tm, peer(p)))
 
-    for p in range(1, heads_axis):
-        x_copy(p).start()
     for m in range(5):
+        own[m].wait()
 
         @pl.when(z < zs - 1)
         def _():
@@ -153,6 +158,9 @@
 
         across(m, z).start()
         if m == 0:
+            own[5].wait()
+            for p in range(1, heads_axis):
+                x_copy(p).start()
             for p in range(1, heads_axis):
                 plane(z, p).start()
 
@@ -165,17 +173,27 @@
         run_col = jnp.sum(jnp.where(at_row == at_col, run_row, 0.0), axis=1, keepdims=True)
         runs[h] = jnp.broadcast_to(run_col, (length, HEAD_DIM))
         decay[h] = jnp.exp(jnp.where(at_row >= at_col, run_col - run_row, -jnp.inf))
-    for p in range(1, heads_axis):
-        at = peer(p)
-        ref = x.at[pl.ds(pl.multiple_of(at * frames_here, frames_here), frames_here), :]
-        remote(ref, ref, x_send.at[p], x_recv.at[at], sibling).wait_recv()
+    def frames_landed():
+        for p in range(1, heads_axis):
+            at = peer(p)
+            ref = x.at[pl.ds(pl.multiple_of(at * frames_here, frames_here), frames_here), :]
+            remote(ref, ref, x_send.at[p], x_recv.at[at], sibling).wait_recv()
 
     def lap(d, _):
         for m in range(5):
             pass_on(m, d)
-            if m > 0:
-                project(m, d - 1)
-        plane_pass_on(d - 1)
+
+        @pl.when(d == 1)
+        def _():
+            frames_landed()
+
+        for m in range(1, 5):
+            project(m, d - 1)
+
+        @pl.when(d > 1)
+        def _():
+            plane_pass_on(d - 2)
+
         return 0
 
     lax.fori_loop(1, zs - 1, lap, 0)
@@ -238,8 +256,9 @@
         scores = lax.dot_general(query, key, (((1,), (1,)), ((), ())), preferred_element_type=F32)
         weights = (scores * decay[h]).astype(BF16)
         ret[:, columns_of(h)] = jnp.dot(weights, value, preferred_element_type=F32)
+    pass_on(4, zs - 1)
+    plane_pass_on(zs - 3)
     plane_pass_on(zs - 2)
-    pass_on(4, zs - 1)
     project(4, zs - 2)
 
     @pl.when(jnp.logical_and(c == 1, z > 0))
@@ -374,13 +393,15 @@
         rows, width = w_query.shape
         length, heads = log_decay.shape
         vmem = pl.BlockSpec(memory_space=pltpu.VMEM)
+        hbm = pl.BlockSpec(memory_space=pltpu.HBM)
         dma = pltpu.SemaphoreType.DMA
         return pl.pallas_call(
             functools.partial(kernel, tms, heads_axis),
             out_shape=jax.ShapeDtypeStruct((here, model), BF16),
-            in_specs=[vmem] * 7,
+            in_specs=[hbm, vmem] + [hbm] * 5,
             out_specs=vmem,
             scratch_shapes=[
+                dma((6,)),
                 pltpu.VMEM((length, model), BF16),
                 pltpu.VMEM((4, tms, rows, width), BF16),
                 pltpu.VMEM((heads_axis, tms) + w_out.shape, BF16),

time: 112 us -> 112 us (level)
  no operation moved by 1% of the time
where the time goes in v2:
time: 112 us
  Pallas kernels  105 us (94%)
  local copies, waits for them, and re-layouts  6.59 us (6%)
    pallas_call x1, Pallas kernels, shards(): pl.pallas_call(functools.partial(kernel, tms, heads_axis), out_shape=jax....  105 us
    unnamed x14, local copies, waits for them, and re-layouts  6.59 us

profile of v2, /device:TPU:29, one launch (start us, length us, event | category | flops | bytes accessed | tf_op | source)
XLA Modules:
  0.0 111.9 jit_solution(11383923947095134552)
XLA Ops:
  0.0 0.0 copy-start.1
  0.0 0.9 copy.8.ld_ref
  0.9 0.1 copy-done.1
  1.0 0.0 copy-start
  1.0 1.0 copy-done
  2.0 0.0 copy-start.2
  2.0 0.9 copy-done.2
  3.0 0.0 copy-start.3
  3.0 0.9 copy-done.3
  3.9 0.0 copy-start.4
  3.9 0.9 copy-done.4
  4.9 0.0 copy-start.5
  4.9 0.9 copy-done.5
  5.8 105.3 %shard_map.73 = bf16[128,2048]{1,0:T(8,128)(2,1)S(1)} custom-call(bf16[128,2048]{1,0:T(8,128)(2,1)S(1)} %copy-done, f32[512,4]{1,0:T(8,128)S(1)} %copy.8.ld_ref, bf16[256,512]{1,0:T(8,128)(2,1)S(1)} %copy-done.1, bf16[256,512]{1,0:T(8,128)(2,1)S(1)} %copy-done.2, bf16[256,512]{1,0:T(8,128)(2,1)S(1)} %copy-done.3, bf16[256,512]{1,0:T(8,128)(2,1)S(1)} %copy-done.4, ...), custom_call_target="tpu_custom_call" | custom-call | tf_op jit(solution)/shard_map/pallas_call | solution.py:398
  111.1 0.8 copy.10
Async XLA Ops:
  0.0 1.0 copy-start.1
  1.0 1.0 copy-start
  2.0 0.9 copy-start.2
  3.0 0.9 copy-start.3
  3.9 0.9 copy-start.4
  4.9 0.9 copy-start.5

commit v3 on v2

--- a/solution.py
+++ b/solution.py
@@ -15,7 +15,7 @@
 
 def kernel(
     tms, heads_axis, x_ref, ld_ref, wk_ref, wv_ref, wq_ref, wg_ref, wo_ref, out_ref,
-    in_sem, x, w, wo, acc, decay, runs, sown, sprev, rin, rout, ret, gated, owned,
+    total, in_sem, x, w, wo, acc, decay, runs, sown, sprev, rin, rout, ret, gated, owned,
     x_send, x_recv, w_send, w_recv, o_recv, oxy_send, osib_send,
     s_send, s_recv, r_send, r_recv, rs_send, g_send, g_recv,
 ):
@@ -89,6 +89,8 @@
 
             @pl.when(jnp.logical_and(to >= 0, to < zs))
             def _():
+                if m >= 2:
+                    along(m - 2, zo, side).wait_send()
                 along(m, zo, side).start()
 
             across(m, zo).start()
@@ -168,9 +170,9 @@
     at_row = lax.broadcasted_iota(jnp.int32, (length, length), 0)
     at_col = lax.broadcasted_iota(jnp.int32, (length, length), 1)
     for h in range(heads):
-        steps = ld_ref[:, h : h + 1]
-        run_row = jnp.sum(jnp.where(at_row <= at_col, steps, 0.0), axis=0, keepdims=True)
-        run_col = jnp.sum(jnp.where(at_row == at_col, run_row, 0.0), axis=1, keepdims=True)
+        steps = ld_ref[h : h + 1, :]
+        run_col = jnp.sum(jnp.where(at_row >= at_col, steps, 0.0), axis=1, keepdims=True)
+        run_row = jnp.sum(jnp.where(at_row == at_col, run_col, 0.0), axis=0, keepdims=True)
         runs[h] = jnp.broadcast_to(run_col, (length, HEAD_DIM))
         decay[h] = jnp.exp(jnp.where(at_row >= at_col, run_col - run_row, -jnp.inf))
     def frames_landed():
@@ -328,20 +330,24 @@
         return 0
 
     lax.fori_loop(0, zs, all_out, 0)
-    for p in range(1, heads_axis):
+    wide = wo_ref.shape[1]
+    for p in range(heads_axis):
         at = peer(p)
-        remote(owned.at[at], owned.at[at], g_send.at[p], g_recv.at[at], sibling).wait_recv()
-
-    wide = wo_ref.shape[1]
-
-    def finish(t, _):
-        total = jnp.zeros((frames_here, wide), F32)
-        for at in range(heads_axis):
-            total += jnp.dot(owned[at], wo[at, t], preferred_element_type=F32)
-        out_ref[:, pl.ds(pl.multiple_of(t * wide, wide), wide)] = total.astype(BF16)
-        return 0
-
-    lax.fori_loop(0, tms, finish, 0)
+        if p > 0:
+            remote(owned.at[at], owned.at[at], g_send.at[p], g_recv.at[at], sibling).wait_recv()
+
+        def finish(t, _):
+            here = pl.ds(pl.multiple_of(t * wide, wide), wide)
+            part = jnp.dot(owned[at], wo[at, t], preferred_element_type=F32)
+            if p > 0:
+                part += total[:, here]
+            if p < heads_axis - 1:
+                total[:, here] = part
+            else:
+                out_ref[:, here] = part.astype(BF16)
+            return 0
+
+        lax.fori_loop(0, tms, finish, 0)
 
     for p in range(1, heads_axis):
         x_copy(p).wait_send()
@@ -368,11 +374,13 @@
         for m in range(5):
             across(m, zo).wait_send()
 
-            @pl.when(jnp.logical_and(zo <= z, z < zs - 1))
+            right, left = (zo <= z, zo >= z) if m >= 3 else (zo == z, zo == z)
+
+            @pl.when(jnp.logical_and(right, z < zs - 1))
             def _():
                 along(m, zo, 0).wait_send()
 
-            @pl.when(jnp.logical_and(zo >= z, z > 0))
+            @pl.when(jnp.logical_and(left, z > 0))
             def _():
                 along(m, zo, 1).wait_send()
 
@@ -401,6 +409,7 @@
             in_specs=[hbm, vmem] + [hbm] * 5,
             out_specs=vmem,
             scratch_shapes=[
+                pltpu.VMEM((here, model), F32),
                 dma((6,)),
                 pltpu.VMEM((length, model), BF16),
                 pltpu.VMEM((4, tms, rows, width), BF16),
@@ -431,9 +440,9 @@
                 dma((heads_axis,)),
             ],
             compiler_params=pltpu.CompilerParams(
-                collective_id=0, has_side_effects=True, vmem_limit_bytes=50 * 2**20
+                collective_id=0, has_side_effects=True, vmem_limit_bytes=62 * 2**20
             ),
-        )(frames, log_decay, w_key, w_value, w_query, w_gate, w_out)
+        )(frames, log_decay.T, w_key, w_value, w_query, w_gate, w_out)
 
     return jax.shard_map(
         shards,

time: 112 us -> 111 us (level); the launches traced: 112 us -> 110 us
  local copies, waits for them, and re-layouts: 6.59 us -> 1.88 us
  Pallas kernels: 105 us -> 108 us
    unnamed x14 -> x1, local copies, waits for them, and re-layouts: 6.59 us -> 1.88 us
    pallas_call x1, Pallas kernels: 105 us -> 108 us  [shards(): pl.pallas_call(functools.partial(kernel, tms, heads_axis), out_shape=jax....]
where the time goes in v3:
time: 111 us; the launch traced here: 110 us
  Pallas kernels  108 us (97%)
  local copies, waits for them, and re-layouts  1.88 us (2%)
    pallas_call x1, Pallas kernels, shards(): pl.pallas_call(functools.partial(kernel, tms, heads_axis), out_shape=jax....  108 us

profile of v3, /device:TPU:29, one launch (start us, length us, event | category | flops | bytes accessed | tf_op | source)
XLA Modules:
  0.0 109.6 jit_solution(4421497973710053367)
XLA Ops:
  0.0 107.7 %shard_map.73 = bf16[128,2048]{1,0:T(8,128)(2,1)} custom-call(bf16[128,2048]{1,0:T(8,128)(2,1)} %x_ref.1, f32[4,512]{1,0:T(4,128)} %bitcast.1, bf16[256,512]{1,0:T(8,128)(2,1)} %wk_ref.1, bf16[256,512]{1,0:T(8,128)(2,1)} %wv_ref.1, bf16[256,512]{1,0:T(8,128)(2,1)} %wq_ref.1, bf16[256,512]{1,0:T(8,128)(2,1)} %wg_ref.1, bf16[512,256]{1,0:T(8,128)(2,1)} %wo_ref.1), custom_call_target="tpu_custom_call" | custom-call | tf_op jit(solution)/shard_map/pallas_call | solution.py:406
  107.7 1.9 %copy.9 = bf16[128,2048]{1,0:T(8,128)(2,1)} copy(bf16[128,2048]{1,0:T(8,128)(2,1)} %shard_map.73) | data formatting | bytes 1048576

commit v4 on v3

--- a/solution.py
+++ b/solution.py
@@ -89,8 +89,6 @@
 
             @pl.when(jnp.logical_and(to >= 0, to < zs))
             def _():
-                if m >= 2:
-                    along(m - 2, zo, side).wait_send()
                 along(m, zo, side).start()
 
             across(m, zo).start()
@@ -303,6 +301,7 @@
         spread = jnp.mean(centred * centred, axis=1, keepdims=True)
         ret[:, columns_of(h)] = centred * lax.rsqrt(spread + 1e-05)
 
+    plane_pass_on(zs - 1)
     project(4, zs - 1)
 
     def g_copy(p):
@@ -321,8 +320,6 @@
         gated[part, :] = gate_rows(at)
         g_copy(p).start()
     owned[hd] = gate_rows(hd)
-
-    plane_pass_on(zs - 1)
 
     def all_out(zo, _):
         for at in range(heads_axis):
@@ -374,13 +371,11 @@
         for m in range(5):
             across(m, zo).wait_send()
 
-            right, left = (zo <= z, zo >= z) if m >= 3 else (zo == z, zo == z)
-
-            @pl.when(jnp.logical_and(right, z < zs - 1))
+            @pl.when(jnp.logical_and(zo <= z, z < zs - 1))
             def _():
                 along(m, zo, 0).wait_send()
 
-            @pl.when(jnp.logical_and(left, z > 0))
+            @pl.when(jnp.logical_and(zo >= z, z > 0))
             def _():
                 along(m, zo, 1).wait_send()
 

time: 111 us -> 111 us (level)
  no operation moved by 1% of the time
where the time goes in v4:
time: 111 us; the launch traced here: 110 us
  Pallas kernels  108 us (97%)
  local copies, waits for them, and re-layouts  1.88 us (2%)
    pallas_call x1, Pallas kernels, shards(): pl.pallas_call(functools.partial(kernel, tms, heads_axis), out_shape=jax....  108 us

profile of v4, /device:TPU:29, one launch (start us, length us, event | category | flops | bytes accessed | tf_op | source)
XLA Modules:
  0.0 109.7 jit_solution(13469072095691032672)
XLA Ops:
  0.0 107.8 %shard_map.73 = bf16[128,2048]{1,0:T(8,128)(2,1)} custom-call(bf16[128,2048]{1,0:T(8,128)(2,1)} %x_ref.1, f32[4,512]{1,0:T(4,128)} %bitcast.1, bf16[256,512]{1,0:T(8,128)(2,1)} %wk_ref.1, bf16[256,512]{1,0:T(8,128)(2,1)} %wv_ref.1, bf16[256,512]{1,0:T(8,128)(2,1)} %wq_ref.1, bf16[256,512]{1,0:T(8,128)(2,1)} %wg_ref.1, bf16[512,256]{1,0:T(8,128)(2,1)} %wo_ref.1), custom_call_target="tpu_custom_call" | custom-call | tf_op jit(solution)/shard_map/pallas_call | solution.py:401
  107.8 1.9 %copy.9 = bf16[128,2048]{1,0:T(8,128)(2,1)} copy(bf16[128,2048]{1,0:T(8,128)(2,1)} %shard_map.73) | data formatting | bytes 1048576

commit v5 on v4

--- a/solution.py
+++ b/solution.py
@@ -182,25 +182,21 @@
     def lap(d, _):
         for m in range(5):
             pass_on(m, d)
-
-        @pl.when(d == 1)
-        def _():
-            frames_landed()
-
+        return 0
+
+    lax.fori_loop(1, zs - 1, lap, 0)
+    frames_landed()
+
+    def products(d, _):
         for m in range(1, 5):
-            project(m, d - 1)
-
-        @pl.when(d > 1)
-        def _():
-            plane_pass_on(d - 2)
-
+            project(m, d)
+        plane_pass_on(d)
         return 0
 
-    lax.fori_loop(1, zs - 1, lap, 0)
+    lax.fori_loop(0, zs - 1, products, 0)
     for m in range(3):
         pass_on(m, zs - 1)
         if m > 0:
-            project(m, zs - 2)
             project(m, zs - 1)
 
     def columns_of(h):
@@ -247,7 +243,6 @@
             next_copy(h).start()
 
     pass_on(3, zs - 1)
-    project(3, zs - 2)
     project(3, zs - 1)
     for h in range(heads):
         query = acc[2, :, columns_of(h)].astype(BF16)
@@ -257,9 +252,6 @@
         weights = (scores * decay[h]).astype(BF16)
         ret[:, columns_of(h)] = jnp.dot(weights, value, preferred_element_type=F32)
     pass_on(4, zs - 1)
-    plane_pass_on(zs - 3)
-    plane_pass_on(zs - 2)
-    project(4, zs - 2)
 
     @pl.when(jnp.logical_and(c == 1, z > 0))
     def _():

time: 111 us -> 111 us (level)
  no operation moved by 1% of the time
where the time goes in v5:
time: 111 us; the launch traced here: 110 us
  Pallas kernels  108 us (97%)
  local copies, waits for them, and re-layouts  1.88 us (2%)
    pallas_call x1, Pallas kernels, shards(): pl.pallas_call(functools.partial(kernel, tms, heads_axis), out_shape=jax....  108 us

profile of v5, /device:TPU:29, one launch (start us, length us, event | category | flops | bytes accessed | tf_op | source)
XLA Modules:
  0.0 109.7 jit_solution(4244527743537379907)
XLA Ops:
  0.0 107.8 %shard_map.73 = bf16[128,2048]{1,0:T(8,128)(2,1)} custom-call(bf16[128,2048]{1,0:T(8,128)(2,1)} %x_ref.1, f32[4,512]{1,0:T(4,128)} %bitcast.1, bf16[256,512]{1,0:T(8,128)(2,1)} %wk_ref.1, bf16[256,512]{1,0:T(8,128)(2,1)} %wv_ref.1, bf16[256,512]{1,0:T(8,128)(2,1)} %wq_ref.1, bf16[256,512]{1,0:T(8,128)(2,1)} %wg_ref.1, bf16[512,256]{1,0:T(8,128)(2,1)} %wo_ref.1), custom_call_target="tpu_custom_call" | custom-call | tf_op jit(solution)/shard_map/pallas_call | solution.py:393
  107.8 1.9 %copy.9 = bf16[128,2048]{1,0:T(8,128)(2,1)} copy(bf16[128,2048]{1,0:T(8,128)(2,1)} %shard_map.73) | data formatting | bytes 1048576

commit v6 on v5

--- a/solution.py
+++ b/solution.py
@@ -28,6 +28,12 @@
     frames_here = x_ref.shape[0]
     length = frames_here * heads_axis
     heads = width // HEAD_DIM
+    parts = 2 if heads % 2 == 0 else 1
+    part_width = width // parts
+    kinds = 4 + parts
+
+    def gate_columns(part):
+        return slice(part * part_width, (part + 1) * part_width)
 
     def peer(p):
         return lax.rem(hd + p, heads_axis)
@@ -41,6 +47,8 @@
     def slot(m, position):
         if m == 0:
             return wo.at[hd, position], o_recv.at[hd, position]
+        if m >= 4:
+            return w.at[3, position, :, gate_columns(m - 4)], w_recv.at[m - 1, position]
         return w.at[m - 1, position], w_recv.at[m - 1, position]
 
     def along(m, zo, side):
@@ -102,8 +110,10 @@
         def body(zo, side):
             landed(m, 2 * zo + 1 - c)
             columns = pl.ds(pl.multiple_of(zo * (2 * rows), 2 * rows), 2 * rows)
-            block = w[m - 1, pl.ds(2 * zo, 2)].reshape(2 * rows, width)
-            acc[m - 1] += jnp.dot(x[:, columns], block, preferred_element_type=F32)
+            out = gate_columns(m - 4) if m >= 4 else slice(0, width)
+            at = min(m - 1, 3)
+            block = w[at, pl.ds(2 * zo, 2), :, out].reshape(2 * rows, out.stop - out.start)
+            acc[at, :, out] += jnp.dot(x[:, columns], block, preferred_element_type=F32)
 
         both(d, body)
 
@@ -145,8 +155,9 @@
     def x_copy(p):
         return remote(x.at[here, :], x.at[here, :], x_send.at[p], x_recv.at[hd], (tm, peer(p)))
 
-    for m in range(5):
-        own[m].wait()
+    for m in range(kinds):
+        if m < 5:
+            own[m].wait()
 
         @pl.when(z < zs - 1)
         def _():
@@ -180,7 +191,7 @@
             remote(ref, ref, x_send.at[p], x_recv.at[at], sibling).wait_recv()
 
     def lap(d, _):
-        for m in range(5):
+        for m in range(kinds):
             pass_on(m, d)
         return 0
 
@@ -188,7 +199,7 @@
     frames_landed()
 
     def products(d, _):
-        for m in range(1, 5):
+        for m in range(1, kinds):
             project(m, d)
         plane_pass_on(d)
         return 0
@@ -294,24 +305,29 @@
         ret[:, columns_of(h)] = centred * lax.rsqrt(spread + 1e-05)
 
     plane_pass_on(zs - 1)
-    project(4, zs - 1)
-
-    def g_copy(p):
-        at = peer(p)
-        piece = gated.at[pl.ds(pl.multiple_of(at * frames_here, frames_here), frames_here), :]
-        return remote(piece, owned.at[hd], g_send.at[p], g_recv.at[hd], (tm, at))
-
-    def gate_rows(at):
-        part = pl.ds(pl.multiple_of(at * frames_here, frames_here), frames_here)
-        gate = acc[3, part, :]
-        return (gate / (1.0 + jnp.exp(-gate)) * ret[part, :]).astype(BF16)
-
-    for p in range(1, heads_axis):
-        at = peer(p)
-        part = pl.ds(pl.multiple_of(at * frames_here, frames_here), frames_here)
-        gated[part, :] = gate_rows(at)
-        g_copy(p).start()
-    owned[hd] = gate_rows(hd)
+    def rows_of(at):
+        return pl.ds(pl.multiple_of(at * frames_here, frames_here), frames_here)
+
+    def g_copy(p, part):
+        at, out = peer(p), gate_columns(part)
+        return remote(
+            gated.at[rows_of(at), out], owned.at[hd, :, out],
+            g_send.at[p, part], g_recv.at[hd, part], (tm, at),
+        )
+
+    def gate_rows(at, part):
+        out = gate_columns(part)
+        gate = acc[3, rows_of(at), out]
+        return (gate / (1.0 + jnp.exp(-gate)) * ret[rows_of(at), out]).astype(BF16)
+
+    for part in range(parts):
+        if part > 0:
+            pass_on(4 + part, zs - 1)
+        project(4 + part, zs - 1)
+        for p in range(1, heads_axis):
+            gated[rows_of(peer(p)), gate_columns(part)] = gate_rows(peer(p), part)
+            g_copy(p, part).start()
+        owned[hd, :, gate_columns(part)] = gate_rows(hd, part)
 
     def all_out(zo, _):
         for at in range(heads_axis):
@@ -320,27 +336,29 @@
 
     lax.fori_loop(0, zs, all_out, 0)
     wide = wo_ref.shape[1]
-    for p in range(heads_axis):
-        at = peer(p)
-        if p > 0:
-            remote(owned.at[at], owned.at[at], g_send.at[p], g_recv.at[at], sibling).wait_recv()
+    for part in range(parts):
+        out = gate_columns(part)
+        for p in range(1, heads_axis):
+            ref = owned.at[peer(p), :, out]
+            remote(ref, ref, g_send.at[p, part], g_recv.at[peer(p), part], sibling).wait_recv()
 
         def finish(t, _):
             here = pl.ds(pl.multiple_of(t * wide, wide), wide)
-            part = jnp.dot(owned[at], wo[at, t], preferred_element_type=F32)
-            if p > 0:
-                part += total[:, here]
-            if p < heads_axis - 1:
-                total[:, here] = part
+            piece = jnp.zeros((frames_here, wide), F32) if part == 0 else total[:, here]
+            for at in range(heads_axis):
+                piece += jnp.dot(owned[at, :, out], wo[at, t, out, :], preferred_element_type=F32)
+            if part < parts - 1:
+                total[:, here] = piece
             else:
-                out_ref[:, here] = part.astype(BF16)
+                out_ref[:, here] = piece.astype(BF16)
             return 0
 
         lax.fori_loop(0, tms, finish, 0)
 
     for p in range(1, heads_axis):
         x_copy(p).wait_send()
-        g_copy(p).wait_send()
+        for part in range(parts):
+            g_copy(p, part).wait_send()
 
     @pl.when(c == 0)
     def _():
@@ -360,7 +378,7 @@
                 share_copy(h).wait_send()
 
     def drain(zo, _):
-        for m in range(5):
+        for m in range(kinds):
             across(m, zo).wait_send()
 
             @pl.when(jnp.logical_and(zo <= z, z < zs - 1))
@@ -413,8 +431,8 @@
                 pltpu.VMEM((heads_axis, here, width), BF16),
                 dma((heads_axis,)),
                 dma((heads_axis,)),
-                dma((5, zs, 3)),
-                dma((4, tms)),
+                dma((6, zs, 3)),
+                dma((5, tms)),
                 dma((heads_axis, tms)),
                 dma((zs, heads_axis)),
                 dma((zs, heads_axis)),
@@ -423,8 +441,8 @@
                 dma((heads,)),
                 dma((heads,)),
                 dma((heads,)),
-                dma((heads_axis,)),
-                dma((heads_axis,)),
+                dma((heads_axis, 2)),
+                dma((heads_axis, 2)),
             ],
             compiler_params=pltpu.CompilerParams(
                 collective_id=0, has_side_effects=True, vmem_limit_bytes=62 * 2**20

time: 111 us -> 109 us (0.982)
  Pallas kernels: 108 us -> 106 us
    pallas_call x1, Pallas kernels: 108 us -> 106 us  [shards(): pl.pallas_call(functools.partial(kernel, tms, heads_axis), out_shape=jax....]
where the time goes in v6:
time: 109 us; the launch traced here: 108 us
  Pallas kernels  106 us (97%)
  local copies, waits for them, and re-layouts  1.88 us (2%)
    pallas_call x1, Pallas kernels, shards(): pl.pallas_call(functools.partial(kernel, tms, heads_axis), out_shape=jax....  106 us

profile of v6, /device:TPU:29, one launch (start us, length us, event | category | flops | bytes accessed | tf_op | source)
XLA Modules:
  0.0 108.2 jit_solution(10232611025002479044)
XLA Ops:
  0.0 106.3 %shard_map.73 = bf16[128,2048]{1,0:T(8,128)(2,1)} custom-call(bf16[128,2048]{1,0:T(8,128)(2,1)} %x_ref.1, f32[4,512]{1,0:T(4,128)} %bitcast.1, bf16[256,512]{1,0:T(8,128)(2,1)} %wk_ref.1, bf16[256,512]{1,0:T(8,128)(2,1)} %wv_ref.1, bf16[256,512]{1,0:T(8,128)(2,1)} %wq_ref.1, bf16[256,512]{1,0:T(8,128)(2,1)} %wg_ref.1, bf16[512,256]{1,0:T(8,128)(2,1)} %wo_ref.1), custom_call_target="tpu_custom_call" | custom-call | tf_op jit(solution)/shard_map/pallas_call | solution.py:411
  106.3 1.9 %copy.9 = bf16[128,2048]{1,0:T(8,128)(2,1)} copy(bf16[128,2048]{1,0:T(8,128)(2,1)} %shard_map.73) | data formatting | bytes 1048576

commit v7 on v6

--- a/solution.py
+++ b/solution.py
@@ -31,6 +31,7 @@
     parts = 2 if heads % 2 == 0 else 1
     part_width = width // parts
     kinds = 4 + parts
+    order = (1, 2, 0) + tuple(range(3, kinds))
 
     def gate_columns(part):
         return slice(part * part_width, (part + 1) * part_width)
@@ -155,7 +156,7 @@
     def x_copy(p):
         return remote(x.at[here, :], x.at[here, :], x_send.at[p], x_recv.at[hd], (tm, peer(p)))
 
-    for m in range(kinds):
+    for m in order:
         if m < 5:
             own[m].wait()
 
@@ -191,7 +192,7 @@
             remote(ref, ref, x_send.at[p], x_recv.at[at], sibling).wait_recv()
 
     def lap(d, _):
-        for m in range(kinds):
+        for m in order:
             pass_on(m, d)
         return 0
 
@@ -205,10 +206,9 @@
         return 0
 
     lax.fori_loop(0, zs - 1, products, 0)
-    for m in range(3):
+    for m in (1, 2):
         pass_on(m, zs - 1)
-        if m > 0:
-            project(m, zs - 1)
+        project(m, zs - 1)
 
     def columns_of(h):
         return slice(h * HEAD_DIM, (h + 1) * HEAD_DIM)
@@ -253,6 +253,7 @@
             state_step(h)
             next_copy(h).start()
 
+    pass_on(0, zs - 1)
     pass_on(3, zs - 1)
     project(3, zs - 1)
     for h in range(heads):
@@ -304,7 +305,6 @@
         spread = jnp.mean(centred * centred, axis=1, keepdims=True)
         ret[:, columns_of(h)] = centred * lax.rsqrt(spread + 1e-05)
 
-    plane_pass_on(zs - 1)
     def rows_of(at):
         return pl.ds(pl.multiple_of(at * frames_here, frames_here), frames_here)
 
@@ -328,6 +328,8 @@
             gated[rows_of(peer(p)), gate_columns(part)] = gate_rows(peer(p), part)
             g_copy(p, part).start()
         owned[hd, :, gate_columns(part)] = gate_rows(hd, part)
+        if part == 0:
+            plane_pass_on(zs - 1)
 
     def all_out(zo, _):
         for at in range(heads_axis):

time: 109 us -> 109 us (level)
  no operation moved by 1% of the time
where the time goes in v7:
time: 109 us
  Pallas kernels  107 us (98%)
  local copies, waits for them, and re-layouts  1.88 us (2%)
    pallas_call x1, Pallas kernels, shards(): pl.pallas_call(functools.partial(kernel, tms, heads_axis), out_shape=jax....  107 us

profile of v7, /device:TPU:29, one launch (start us, length us, event | category | flops | bytes accessed | tf_op | source)
XLA Modules:
  0.0 108.5 jit_solution(3854345787516308586)
XLA Ops:
  0.0 106.6 %shard_map.73 = bf16[128,2048]{1,0:T(8,128)(2,1)} custom-call(bf16[128,2048]{1,0:T(8,128)(2,1)} %x_ref.1, f32[4,512]{1,0:T(4,128)} %bitcast.1, bf16[256,512]{1,0:T(8,128)(2,1)} %wk_ref.1, bf16[256,512]{1,0:T(8,128)(2,1)} %wv_ref.1, bf16[256,512]{1,0:T(8,128)(2,1)} %wq_ref.1, bf16[256,512]{1,0:T(8,128)(2,1)} %wg_ref.1, bf16[512,256]{1,0:T(8,128)(2,1)} %wo_ref.1), custom_call_target="tpu_custom_call" | custom-call | tf_op jit(solution)/shard_map/pallas_call | solution.py:413
  106.6 1.9 %copy.9 = bf16[128,2048]{1,0:T(8,128)(2,1)} copy(bf16[128,2048]{1,0:T(8,128)(2,1)} %shard_map.73) | data formatting | bytes 1048576

commit v8 on v7

--- a/solution.py
+++ b/solution.py
@@ -15,7 +15,7 @@
 
 def kernel(
     tms, heads_axis, x_ref, ld_ref, wk_ref, wv_ref, wq_ref, wg_ref, wo_ref, out_ref,
-    total, in_sem, x, w, wo, acc, decay, runs, sown, sprev, rin, rout, ret, gated, owned,
+    total, in_sem, x, w, wo, acc, decay, runs, sown, sprev, rin, rnext, rout, ret, gated, owned,
     x_send, x_recv, w_send, w_recv, o_recv, oxy_send, osib_send,
     s_send, s_recv, r_send, r_recv, rs_send, g_send, g_recv,
 ):
@@ -217,15 +217,15 @@
         return remote(sown.at[h], sprev.at[h], s_send.at[h], s_recv.at[h], sibling)
 
     def next_copy(h):
-        return remote(rout.at[h], rin.at[h], r_send.at[h], r_recv.at[h], (tm + 2, hd))
+        return remote(rnext.at[h], rin.at[h], r_send.at[h], r_recv.at[h], (tm + 2, hd))
 
     def share_copy(h):
         return remote(rin.at[h], rin.at[h], rs_send.at[h], r_recv.at[h], sibling)
 
     def state_step(h):
-        prior = jnp.exp(sprev[h, HEAD_DIM : HEAD_DIM + 1, :]) * rin[h] + sprev[h, :HEAD_DIM, :]
-        rout[h] = jnp.exp(sown[h, HEAD_DIM : HEAD_DIM + 1, :]) * prior + sown[h, :HEAD_DIM, :]
-        return prior
+        prior = jnp.exp(sprev[h, HEAD_DIM : HEAD_DIM + 1, :]) * rin[h].astype(F32) + sprev[h, :HEAD_DIM, :]
+        later = jnp.exp(sown[h, HEAD_DIM : HEAD_DIM + 1, :]) * prior + sown[h, :HEAD_DIM, :]
+        rnext[h] = later.astype(BF16)
 
     @pl.when(z == 0)
     def _():
@@ -288,18 +288,18 @@
 
         @pl.when(c == 1)
         def _():
-            rout[heads + h] = (
-                jnp.exp(sprev[h, HEAD_DIM : HEAD_DIM + 1, :]) * rin[h] + sprev[h, :HEAD_DIM, :]
+            rout[h] = (
+                jnp.exp(sprev[h, HEAD_DIM : HEAD_DIM + 1, :]) * rin[h].astype(F32) + sprev[h, :HEAD_DIM, :]
             )
 
         @pl.when(c == 0)
         def _():
-            rout[heads + h] = rin[h]
+            rout[h] = rin[h].astype(F32)
 
         query = acc[2, :, columns_of(h)].astype(BF16)
         lifted = query.astype(F32) * jnp.exp(runs[h])
         both_parts = ret[:, columns_of(h)] + jnp.dot(
-            lifted, rout[heads + h], preferred_element_type=F32, precision=lax.Precision.HIGHEST
+            lifted, rout[h], preferred_element_type=F32, precision=lax.Precision.HIGHEST
         )
         centred = both_parts - jnp.mean(both_parts, axis=1, keepdims=True)
         spread = jnp.mean(centred * centred, axis=1, keepdims=True)
@@ -426,8 +426,9 @@
                 pltpu.VMEM((heads, length, HEAD_DIM), F32),
                 pltpu.VMEM((heads, HEAD_DIM + 8, HEAD_DIM), F32),
                 pltpu.VMEM((heads, HEAD_DIM + 8, HEAD_DIM), F32),
+                pltpu.VMEM((heads, HEAD_DIM, HEAD_DIM), BF16),
+                pltpu.VMEM((heads, HEAD_DIM, HEAD_DIM), BF16),
                 pltpu.VMEM((heads, HEAD_DIM, HEAD_DIM), F32),
-                pltpu.VMEM((2 * heads, HEAD_DIM, HEAD_DIM), F32),
                 pltpu.VMEM((length, width), F32),
                 pltpu.VMEM((length, width), BF16),
                 pltpu.VMEM((heads_axis, here, width), BF16),

time: 109 us -> 108 us (level)
  Pallas kernels: 107 us -> 105 us
    pallas_call x1, Pallas kernels: 107 us -> 105 us  [shards(): pl.pallas_call(functools.partial(kernel, tms, heads_axis), out_shape=jax....]
where the time goes in v8:
time: 108 us; the launch traced here: 107 us
  Pallas kernels  105 us (97%)
  local copies, waits for them, and re-layouts  1.88 us (2%)
    pallas_call x1, Pallas kernels, shards(): pl.pallas_call(functools.partial(kernel, tms, heads_axis), out_shape=jax....  105 us

profile of v8, /device:TPU:29, one launch (start us, length us, event | category | flops | bytes accessed | tf_op | source)
XLA Modules:
  0.0 107.1 jit_solution(1989136918644098383)
XLA Ops:
  0.0 105.2 %shard_map.73 = bf16[128,2048]{1,0:T(8,128)(2,1)} custom-call(bf16[128,2048]{1,0:T(8,128)(2,1)} %x_ref.1, f32[4,512]{1,0:T(4,128)} %bitcast.1, bf16[256,512]{1,0:T(8,128)(2,1)} %wk_ref.1, bf16[256,512]{1,0:T(8,128)(2,1)} %wv_ref.1, bf16[256,512]{1,0:T(8,128)(2,1)} %wq_ref.1, bf16[256,512]{1,0:T(8,128)(2,1)} %wg_ref.1, bf16[512,256]{1,0:T(8,128)(2,1)} %wo_ref.1), custom_call_target="tpu_custom_call" | custom-call | tf_op jit(solution)/shard_map/pallas_call | solution.py:413
  105.2 1.9 %copy.9 = bf16[128,2048]{1,0:T(8,128)(2,1)} copy(bf16[128,2048]{1,0:T(8,128)(2,1)} %shard_map.73) | data formatting | bytes 1048576
